TPU v7x, 128 devices: a whole 4x4x4 slice. The times are simulated.
128 devices in a mesh: dp: 4 (over x), grid: 32 (over y, z, core).
Axes of the slice: x: 4, y: 4, z: 4, core: 2. Of those that a mesh axis runs over, the one named last changes fastest.
Arguments:
- embeddings: bfloat16 [40960, 768], P(('dp', 'grid')), may hold values from -6 to 6
- cluster: int32 [40960, 1], P(('dp', 'grid')), may hold values from 0 to 3; in each aligned block of 320 rows (0 to 319, 320 to 639, ...) at most 160 rows name the same one
- order_key: int32 [40960], P(('dp', 'grid')), may hold values from 0 to 40959, each once
Outputs:
- best: float32 [40960], P(('dp', 'grid'))
Inputs may be any that keep to these rules, and one draw needn't show every extreme that they name: In the rows of one device at most 160 rows name one cluster, and on some device one cluster is named by exactly 160 rows; every cluster is named. `order_key`: each number of 0 to 40959 appears once.
All inputs are finite; a program needn't handle non-finite values.
Results may differ from a plain program's by a relative error of at most 0.0012.
Values may be sent and summed in bfloat16 or wider, within the bound.
A program may use at most 128 MiB of HBM per device.

v0:
```python
import jax
import jax.numpy as jnp
from jax import lax
from jax.sharding import PartitionSpec as P

epsilon = 1e-06


def shards(embeddings, cluster, order_key):
    rows = embeddings.shape[0]
    width = embeddings.shape[1]
    owners = lax.axis_size("dp")
    values = embeddings.astype(jnp.float32)
    units = (values * lax.rsqrt(jnp.sum(values * values, axis=1, keepdims=True) + epsilon)).astype(
        jnp.bfloat16
    )
    labels = cluster[:, 0]
    depth = rows // 2
    onehot = (labels[:, None] == jnp.arange(owners, dtype=jnp.int32)[None, :]).astype(jnp.int32)
    before = jnp.cumsum(onehot, axis=0) - onehot
    places = jnp.sum(before * onehot, axis=1)
    flat = labels * depth + places
    send_units = (
        jnp.zeros((owners * depth, width), jnp.bfloat16)
        .at[flat]
        .set(units)
        .reshape(owners, depth, width)
    )
    send_keys = (
        jnp.full((owners * depth,), -1, jnp.int32).at[flat].set(order_key).reshape(owners, depth)
    )
    got_units, got_keys = (
        lax.all_to_all(send_units, "dp", split_axis=0, concat_axis=0, tiled=True),
        lax.all_to_all(send_keys, "dp", split_axis=0, concat_axis=0, tiled=True),
    )
    mine = got_units.reshape(owners * depth, width)
    mine_keys = got_keys.reshape(owners * depth)
    initial = jnp.full((owners * depth,), -1.0, jnp.float32)
    other_units = lax.all_gather(mine, "grid", axis=0, tiled=True)
    other_keys = lax.all_gather(mine_keys, "grid", axis=0, tiled=True)
    sims = jnp.einsum("qe,ke->qk", mine, other_units, preferred_element_type=jnp.float32)
    allowed = (other_keys[None, :] >= 0) & (other_keys[None, :] < mine_keys[:, None])
    scores = jnp.maximum(initial, jnp.max(jnp.where(allowed, sims, jnp.float32(-1.0)), axis=1))
    returned = lax.all_to_all(
        scores.reshape(owners, depth), "dp", split_axis=0, concat_axis=0, tiled=True
    )
    return returned.reshape(owners * depth)[flat]


def solution(mesh):
    placed = (P(("dp", "grid"), None), P(("dp", "grid"), None), P(("dp", "grid")))
    return jax.shard_map(
        shards, mesh=mesh, in_specs=placed, out_specs=P(("dp", "grid")), check_vma=False
    )
```

profile of v0, /device:TPU:1, one launch (start us, length us, event | category | flops | bytes accessed | tf_op | source)
XLA Modules:
  0.0 188.9 jit_solution(2307655279591229633)
XLA Ops:
  6.5 0.0 all-gather.3.cloned.1.call-start
  6.5 0.7 reduce
  7.3 1.2 reduce-window.6
  8.5 0.2 slice_reduce_fusion
  8.7 0.2 reduce-window.9
  8.9 0.1 add_bitcast_fusion
  9.0 0.7 fusion.10
  9.7 1.2 fusion
  10.9 2.8 %scatter_custom_fusion.1 = bf16[640,768]{1,0:T(8,128)(2,1)S(1)} fusion(s32[320]{0:T(512)S(1)} %fusion.10, bf16[320,768]{1,0:T(8,128)(2,1)} %param.3, f32[320]{0:T(512)S(1)} %add_rsqrt_fusion, bf16[]{:T(256)} %constant.6.clone.1), kind=kCustom, calls=%fused_computation.8 | custom fusion | flops 737280 | bytes 1476610 | tf_op jit(solution)/shard_map/scatter | solution.py:26
  13.7 17.9 %all_to_all.20 = bf16[4,160,768]{2,1,0:T(8,128)(2,1)} all-to-all(bf16[4,160,768]{2,1,0:T(8,128)(2,1)S(1)} %bitcast.18), channel_id=1, replica_groups=mesh['dp'=4,'grid'=32] {'dp'}, dimensions={0} | all-to-all | bytes 1966080 | tf_op jit(solution)/shard_map/all_to_all | solution.py:33
  31.7 0.0 all-gather.3.cloned.1.call-update
  31.7 3.1 %scatter_custom_fusion = s32[640]{0:T(1024)S(1)} fusion(s32[320]{0:T(512)S(1)} %fusion.10, s32[320]{0:T(512)} %param.5, s32[]{:T(128)} %constant.10.clone.1), kind=kCustom, calls=%fused_computation.25 | custom fusion | bytes 3072 | tf_op jit(solution)/shard_map/scatter | solution.py:30
  34.8 0.1 all_to_all.13
  34.9 6.5 %all_to_all.21 = s32[4,1,160]{2,1,0:T(1,128)S(1)} all-to-all(s32[4,1,160]{2,1,0:T(1,128)S(1)} %all_to_all.13), channel_id=1, replica_groups=mesh['dp'=4,'grid'=32] {'dp'}, dimensions={0} | all-to-all | bytes 5120 | tf_op jit(solution)/shard_map/all_to_all | solution.py:34
  41.4 0.1 reshape.88
  41.5 0.1 reshape.59
  41.5 29.0 %all-gather = s32[32,1,640]{2,1,0:T(1,128)S(1)} all-gather(s32[1,1,640]{2,1,0:T(1,128)S(1)} %reshape.88), channel_id=1, replica_groups=mesh['dp'=4,'grid'=32] {'grid'}, dimensions={0}, use_global_device_ids=true | all-gather | bytes 84480 | tf_op jit(solution)/shard_map/all_gather | solution.py:40
  70.5 72.4 %all-gather.3.cloned.1.call-done = bf16[20480,768]{1,0:T(8,128)(2,1)} async-done(((bf16[640,768]{1,0:T(8,128)(2,1)}), bf16[20480,768]{1,0:T(8,128)(2,1)}) %all-gather.3.cloned.1.call-update) | async-done | bytes 31457296 | tf_op jit(solution)/shard_map/all_gather | solution.py:39
  142.9 27.4 %select_reduce_fusion = f32[640]{0:T(1024)S(1)} fusion(bf16[640,768]{1,0:T(8,128)(2,1)} %bitcast.17, bf16[20480,768]{1,0:T(8,128)(2,1)} %all-gather.3.cloned.1.call-done, s32[20480]{0:T(1024)S(1)} %bitcast.20, s32[640]{0:T(1024)S(1)} %reshape.59, pred[20480]{0:T(1024)(128)(4,1)S(1)} %broadcast_compare_fusion), kind=kOutput, calls=%fused_computation.3 | convolution fusion | flops 20185088000 | bytes 32547840 | tf_op jit(solution)/shard_map/qe,ke->qk/dot_general | solution.py:41
  170.3 0.7 max_broadcast_in_dim.15
  171.0 4.0 %all-to-all-start.2 = ((f32[4,1,160]{2,1,0:T(1,128)}), f32[4,1,160]{2,1,0:T(1,128)S(1)}, u32[]{:S(2)}, u32[]{:S(2)}) async-start(f32[4,1,160]{2,1,0:T(1,128)} %max_broadcast_in_dim.15), calls=%async_computation.2 | async-start | bytes 8192 | tf_op jit(solution)/shard_map/all_to_all | solution.py:44
  175.0 4.1 %all-to-all-done.2 = f32[4,1,160]{2,1,0:T(1,128)S(1)} async-done(((f32[4,1,160]{2,1,0:T(1,128)}), f32[4,1,160]{2,1,0:T(1,128)S(1)}, u32[]{:S(2)}, u32[]{:S(2)}) %all-to-all-start.2) | async-done | bytes 2592 | tf_op jit(solution)/shard_map/all_to_all | solution.py:44
  179.1 0.1 reshape.62
  179.2 2.8 %gather_fusion = f32[320]{0:T(512)} fusion(f32[640]{0:T(1024)S(1)} %reshape.62, s32[1024]{0:T(1024)S(1)} %pad_clamp_fusion), kind=kCustom, calls=%fused_computation | custom fusion | bytes 3840 | tf_op jit(solution)/shard_map/gather | solution.py:47
  (11 shorter events, 0.1 us)
Async XLA Ops:
  6.5 136.4 %all-gather.3.cloned.1.call-start = ((), (), s32[]{:S(2)}) async-start(), calls=%async_computation.3 | async-start | bytes 32440320 | tf_op jit(solution)/shard_map/all_gather | solution.py:39
  171.0 8.1 %all-to-all-start.2 = ((f32[4,1,160]{2,1,0:T(1,128)}), f32[4,1,160]{2,1,0:T(1,128)S(1)}, u32[]{:S(2)}, u32[]{:S(2)}) async-start(f32[4,1,160]{2,1,0:T(1,128)} %max_broadcast_in_dim.15), calls=%async_computation.2 | async-start | bytes 8192 | tf_op jit(solution)/shard_map/all_to_all | solution.py:44
Sparse Core Ops, SparseCore 0:
  31.8 111.0 all-gather.2
where the time goes:
time: 190 us; the launch traced here: 189 us
  waiting for transfers between devices  76.5 us (40%)
  blocking collectives  53.4 us (28%)
  matrix products  27.4 us (14%)
  between operations  13.5 us (7%)
  local copies, waits for them, and re-layouts  7.11 us (4%)
  other arithmetic  7.01 us (4%)
  starting transfers between devices  3.96 us (2%)
    all_gather x1, waiting for transfers between devices, shards(): other_units = lax.all_gather(mine, 'grid', axis=0, tiled=True)  72.4 us
    all_gather x1, blocking collectives, shards(): other_keys = lax.all_gather(mine_keys, 'grid', axis=0, tiled=True)  29 us
    dot_general x1, matrix products, shards(): jnp.einsum('qe,ke->qk', mine, other_units, preferred_element_type=jnp.flo...  27.4 us
    all_to_all x1, blocking collectives, shards(): lax.all_to_all(send_units, 'dp', split_axis=0, concat_axis=0, tiled=True)  17.9 us
    all_to_all x1, blocking collectives, shards(): lax.all_to_all(send_keys, 'dp', split_axis=0, concat_axis=0, tiled=True)  6.47 us
    all_to_all x1, waiting for transfers between devices, shards(): lax.all_to_all(scores.reshape(owners, depth), 'dp', split_axis=0, concat_...  4.13 us
    all_to_all x1, starting transfers between devices, shards(): lax.all_to_all(scores.reshape(owners, depth), 'dp', split_axis=0, concat_...  3.96 us
  transfers between devices with their start and end apart: 2, of which 2 were waited for; matrix products, arithmetic and copies ran while one was open for 2% of the time, Pallas kernels for 0%

commit v1 on v0

v1 whole, which is shorter than its diff:
```python
import functools

import jax
import jax.numpy as jnp
from jax import lax
from jax.experimental import pallas as pl
from jax.experimental.pallas import tpu as pltpu
from jax.sharding import PartitionSpec as P

MESH = pl.DeviceIdType.MESH
NT = (((1,), (1,)), ((), ()))
epsilon = 1e-06
scale = 65536.0

OFFSETS = {
    "o": (0, 0, 0), "a": (0, 0, 1), "b": (0, 0, 2), "c": (0, 1, 0), "d": (0, 1, 2), "e": (0, 1, 3),
    "f": (0, 3, 0), "g": (1, 0, 0), "h": (2, 0, 0), "i": (2, 3, 0), "j": (3, 1, 3), "k": (3, 3, 0),
}
FULL = "oacfgkebhd"
HALF = "ij"
BLOCKS = FULL + HALF
SLOT = {b: n for n, b in enumerate(BLOCKS)}
CHUNKS = 5
ONE_WAY = {"oo", "cf", "df", "dc", "di", "bh", "ho", "ic", "id"}
COLUMNS = "acgfekdbh"
RETURNED = "acgfekdbhij"


def kernel(rows, width, x_ref, meta_in, out_ref, full, half, meta, col_c, col_g, acc_row, acc_col, ret, back,
           send, recv, d2d_send, d2d_recv, m_send, m_recv, md_send, md_recv, r_send, r_recv):
    x, grid = lax.axis_index("dp"), lax.axis_index("grid")
    y, z, core = grid // 8, (grid // 2) % 4, grid % 2
    pair_rows = 2 * rows
    step = rows // CHUNKS
    mine = pl.multiple_of(core * rows, step)

    def device(offset, which):
        dx, dy, dz = offset
        return ((x + dx) % 4, ((y + dy) % 4) * 8 + ((z + dz) % 4) * 2 + which)

    def minus(offset):
        return tuple(-v for v in offset)

    sibling = device((0, 0, 0), 1 - core)
    barrier = pltpu.get_barrier_semaphore()
    partners = {((0, 0, 0), 1)}
    for b in BLOCKS[1:]:
        for offset in (OFFSETS[b], tuple(-v % 4 for v in OFFSETS[b])):
            partners.add((offset, 0))
            if b in FULL:
                partners.add((offset, 1))
    neighbours = [device(offset, 1 - core if other else core) for offset, other in sorted(partners)]
    for n in neighbours:
        pl.semaphore_signal(barrier, inc=1, device_id=n, device_id_type=MESH)

    def place(b, s):
        if b in FULL:
            return full.at[SLOT[b], pl.ds(pl.multiple_of(core * rows + s * step, step), step)]
        return half.at[SLOT[b] - len(FULL), pl.ds(s * step, step)]

    pending = []

    def hop(source, target, s):
        offset = tuple((q - p) % 4 for p, q in zip(OFFSETS[source], OFFSETS[target]))
        c = pltpu.make_async_remote_copy(
            src_ref=place(source, s), dst_ref=place(target, s),
            send_sem=send.at[SLOT[target], s], recv_sem=recv.at[SLOT[target], s],
            device_id=device(offset, core), device_id_type=MESH)
        c.start()
        pending.append(c)

    def got(b, s):
        here = place(b, s)
        pltpu.make_async_copy(here, here, recv.at[SLOT[b], s]).wait()

    def meta_hop(source, target):
        offset = tuple((q - p) % 4 for p, q in zip(OFFSETS[source], OFFSETS[target]))
        c = pltpu.make_async_remote_copy(
            src_ref=meta.at[SLOT[source], core], dst_ref=meta.at[SLOT[target], core],
            send_sem=m_send.at[SLOT[target]], recv_sem=m_recv.at[SLOT[target]],
            device_id=device(offset, core), device_id_type=MESH)
        c.start()
        pending.append(c)

    def meta_got(b):
        here = meta.at[SLOT[b], core]
        pltpu.make_async_copy(here, here, m_recv.at[SLOT[b]]).wait()

    def meta_share(b):
        here = meta.at[SLOT[b], core]
        c = pltpu.make_async_remote_copy(
            src_ref=here, dst_ref=here, send_sem=md_send.at[SLOT[b]], recv_sem=md_recv.at[SLOT[b]],
            device_id=sibling, device_id_type=MESH)
        c.start()
        pending.append(c)

    def meta_shared(b):
        here = meta.at[SLOT[b], 1 - core]
        pltpu.make_async_copy(here, here, md_recv.at[SLOT[b]]).wait()

    def share(b, s):
        c = pltpu.make_async_remote_copy(
            src_ref=place(b, s), dst_ref=place(b, s),
            send_sem=d2d_send.at[SLOT[b], s], recv_sem=d2d_recv.at[SLOT[b], s],
            device_id=sibling, device_id_type=MESH)
        c.start()
        pending.append(c)

    def shared(b):
        for s in range(CHUNKS):
            here = full.at[SLOT[b], pl.ds(pl.multiple_of((1 - core) * rows + s * step, step), step)]
            pltpu.make_async_copy(here, here, d2d_recv.at[SLOT[b], s]).wait()

    def columns(b):
        r = meta[SLOT[b], core]
        r = r[:, 0:384] + r[:, 320:704]
        t = jnp.transpose(jnp.broadcast_to(r, (128, 384)))[:rows]
        col_g[SLOT[b]] = t
        col_c[SLOT[b]] = jnp.floor(t * (1.0 / scale))

    def tiles(j, others):
        left = full[SLOT[j], pl.ds(mine, rows), :] if j in FULL else half[SLOT[j] - len(FULL)]
        cj, gj = col_c[SLOT[j]], col_g[SLOT[j]]
        best = acc_row[SLOT[j]]
        for i in others:
            sims = lax.dot_general(left, full[SLOT[i]], NT, preferred_element_type=jnp.float32)
            gi = meta[SLOT[i], 0] + meta[SLOT[i], 1]
            ci = jnp.floor(gi * (1.0 / scale))
            for n in range(0, pair_rows, 128):
                t = jnp.where(cj == ci[:, n:n + 128], sims[:, n:n + 128], -1.0)
                earlier = gi[:, n:n + 128] < gj
                best = jnp.maximum(best, jnp.where(earlier, t, -1.0))
                if j + i not in ONE_WAY:
                    u = jnp.max(jnp.where(earlier, -1.0, t).reshape(rows // 8, 8, 128), axis=0)
                    acc_col[SLOT[i], :, n:n + 128] = jnp.maximum(acc_col[SLOT[i], :, n:n + 128], u)
        acc_row[SLOT[j]] = best

    lanes = lax.broadcasted_iota(jnp.int32, (1, pair_rows), 1)
    ours = (lanes >= core * rows) & (lanes < (core + 1) * rows)

    def summary(b):
        m = jnp.full((1, pair_rows), -1.0, jnp.float32)
        if b not in "f":
            a = acc_row[SLOT[b]]
            a = jnp.concatenate([a, jnp.full((384 - rows, 128), -1.0, jnp.float32)], axis=0)
            r = jnp.max(jnp.transpose(a), axis=0, keepdims=True)[:, :rows]
            m = jnp.where(ours, jnp.concatenate([r, r], axis=1), m)
        if b in COLUMNS:
            m = jnp.maximum(m, jnp.max(acc_col[SLOT[b]], axis=0, keepdims=True))
        return m

    def give(b):
        n = RETURNED.index(b)
        back[n] = summary(b)
        for which in ((0, 1) if b in FULL else (0,)):
            target = core if which == 0 else 1 - core
            c = pltpu.make_async_remote_copy(
                src_ref=back.at[n], dst_ref=ret.at[which, n],
                send_sem=r_send.at[which, n], recv_sem=r_recv.at[which, n],
                device_id=device(minus(OFFSETS[b]), target), device_id_type=MESH)
            c.start()
            pending.append(c)

    values = x_ref[...].astype(jnp.float32)
    units = values * lax.rsqrt(jnp.sum(values * values, axis=1, keepdims=True) + epsilon)
    full[0, pl.ds(mine, rows), :] = units.astype(jnp.bfloat16)
    wide = lax.broadcasted_iota(jnp.int32, (1, 768), 1)
    meta[0, core] = jnp.where((wide >= core * rows) & (wide < (core + 1) * rows), meta_in[...], 0.0)
    pl.semaphore_wait(barrier, len(neighbours))

    for b in "fcag":
        meta_hop("o", b)
    meta_share("o")
    for s in range(CHUNKS):
        for b in "fcag":
            hop("o", b, s)
    for s in range(CHUNKS):
        share("o", s)
    acc_row[...] = jnp.full_like(acc_row, -1.0)
    acc_col[...] = jnp.full_like(acc_col, -1.0)
    columns("o")
    meta_shared("o")
    shared("o")
    for b, children in (("f", "k"), ("c", "ed"), ("a", "b"), ("g", "h")):
        meta_got(b)
        for t in children:
            meta_hop(b, t)
        meta_share(b)
        if b != "f":
            columns(b)
    tiles("o", "o")
    meta_got("e")
    meta_hop("e", "j")
    meta_got("h")
    meta_hop("h", "i")
    meta_share("e")
    meta_share("h")
    for b in "kbd":
        meta_got(b)
        meta_share(b)
    for s in range(CHUNKS):
        got("f", s)
        hop("f", "k", s)
        got("c", s)
        hop("c", "e", s)
        share("f", s)
        share("c", s)
        got("a", s)
        got("g", s)
        share("a", s)
        share("g", s)
        if s >= 3:
            for r in ((0, 1) if s == 3 else (2, 3, 4)):
                hop("a", "b", r)
                hop("g", "h", r)
                if r < 3:
                    hop("c", "d", r)
    for b in "acgf":
        meta_shared(b)
        shared(b)
    tiles("o", "acg")
    for s in range(CHUNKS):
        got("e", s)
        share("e", s)
        hop("e", "j", s)
        if s >= 3:
            hop("e", "d", s)
    tiles("a", "cgf")
    got("h", 0)
    hop("h", "i", 0)
    for s in range(CHUNKS):
        got("k", s)
        share("k", s)
    tiles("g", "cf")
    tiles("c", "f")
    for b in "ek":
        columns(b)
        meta_shared(b)
        shared(b)
    tiles("k", "acge")
    got("h", 1)
    hop("h", "i", 1)
    tiles("e", "fga")
    got("h", 2)
    hop("h", "i", 2)
    columns("d")
    meta_shared("d")
    for s in range(CHUNKS):
        got("d", s)
        share("d", s)
    shared("d")
    tiles("d", "fkgc")
    got("h", 3)
    hop("h", "i", 3)
    columns("b")
    columns("h")
    for b in "bhij":
        if b in "bh":
            meta_shared(b)
        else:
            meta_got(b)
            columns(b)
    got("h", 4)
    hop("h", "i", 4)
    for s in range(CHUNKS):
        share("h", s)
        got("b", s)
        share("b", s)
    shared("b")
    shared("h")
    tiles("b", "gkh")
    tiles("h", "aeod")
    for b in "gkd":
        give(b)
    for s in range(CHUNKS):
        got("j", s)
    tiles("j", "bcfh")
    for s in range(CHUNKS):
        got("i", s)
    tiles("i", "acde")
    for b in "bcfhjaei":
        give(b)
    total = summary("o")
    for c in pending:
        c.wait_send()
    for n, b in enumerate(RETURNED):
        for which in ((0, 1) if b in FULL else (0,)):
            here = ret.at[which, n]
            pltpu.make_async_copy(here, here, r_recv.at[which, n]).wait()
            total = jnp.maximum(total, ret[which, n])
    out_ref[...] = jnp.where(core == 0, total[:, :rows], total[:, rows:])


def shards(embeddings, cluster, order_key):
    rows, width = embeddings.shape
    both = (cluster[:, 0] * 65536 + order_key).astype(jnp.float32)
    both = jnp.concatenate([both, both, jnp.zeros((768 - 2 * rows,), jnp.float32)]).reshape(1, 768)
    nf, nh, nb, nr = len(FULL), len(HALF), len(BLOCKS), len(RETURNED)

    dma = pltpu.SemaphoreType.DMA
    best = pl.pallas_call(
        functools.partial(kernel, rows, width),
        out_shape=jax.ShapeDtypeStruct((1, rows), jnp.float32),
        in_specs=[pl.BlockSpec(memory_space=pltpu.VMEM)] * 2,
        out_specs=pl.BlockSpec(memory_space=pltpu.VMEM),
        scratch_shapes=[
            pltpu.VMEM((nf, 2 * rows, width), jnp.bfloat16),
            pltpu.VMEM((nh, rows, width), jnp.bfloat16),
            pltpu.VMEM((nb, 2, 1, 768), jnp.float32),
            pltpu.VMEM((nb, rows, 128), jnp.float32),
            pltpu.VMEM((nb, rows, 128), jnp.float32),
            pltpu.VMEM((nb, rows, 128), jnp.float32),
            pltpu.VMEM((nf, 8, 2 * rows), jnp.float32),
            pltpu.VMEM((2, nr, 1, 2 * rows), jnp.float32),
            pltpu.VMEM((nr, 1, 2 * rows), jnp.float32),
            dma((nb, CHUNKS)), dma((nb, CHUNKS)), dma((nf, CHUNKS)), dma((nf, CHUNKS)),
            dma((nb,)), dma((nb,)), dma((nf,)), dma((nf,)), dma((2, nr)), dma((2, nr)),
        ],
        compiler_params=pltpu.CompilerParams(
            collective_id=0, has_side_effects=True, vmem_limit_bytes=56 << 20),
        cost_estimate=pl.CostEstimate(
            flops=36 * 2 * rows * 2 * rows * width, bytes_accessed=rows * width * 2, transcendentals=rows),
    )(embeddings, both)
    return best.reshape(rows)


def solution(mesh):
    placed = (P(("dp", "grid"), None), P(("dp", "grid"), None), P(("dp", "grid")))
    return jax.shard_map(
        shards, mesh=mesh, in_specs=placed, out_specs=P(("dp", "grid")), check_vma=False
    )
```

time: 190 us -> 72.9 us (0.38)
  waiting for transfers between devices: 76.5 us -> 0 us
  Pallas kernels: 0 us -> 70.1 us
  blocking collectives: 53.4 us -> 0 us
  matrix products: 27.4 us -> 0 us
  between operations: 13.5 us -> 0.03 us
  local copies, waits for them, and re-layouts: 7.11 us -> 0.61 us
  other arithmetic: 7.01 us -> 2.06 us
  starting transfers between devices: 3.96 us -> 0 us
    all_gather x1 -> x0, waiting for transfers between devices: 72.4 us -> none  [shards(): other_units = lax.all_gather(mine, 'grid', axis=0, tiled=True)]
    pallas_call x0 -> x1, Pallas kernels: none -> 70.1 us  [shards(): pl.pallas_call(functools.partial(kernel, rows, width), out_shape=jax.Shap...]
    all_gather x1 -> x0, blocking collectives: 29 us -> none  [shards(): other_keys = lax.all_gather(mine_keys, 'grid', axis=0, tiled=True)]
    dot_general x1 -> x0, matrix products: 27.4 us -> none  [shards(): jnp.einsum('qe,ke->qk', mine, other_units, preferred_element_type=jnp.flo...]
    all_to_all x2 -> x0, blocking collectives: 24.4 us -> none  [the longest x1 17.9 us: shards(): lax.all_to_all(send_units, 'dp', split_axis=0, concat_axis=0, tiled=True)]
    all_to_all x1 -> x0, waiting for transfers between devices: 4.13 us -> none  [shards(): lax.all_to_all(scores.reshape(owners, depth), 'dp', split_axis=0, concat_...]
    all_to_all x1 -> x0, starting transfers between devices: 3.96 us -> none  [shards(): lax.all_to_all(scores.reshape(owners, depth), 'dp', split_axis=0, concat_...]
    scatter x1 -> x0, local copies, waits for them, and re-layouts: 3.08 us -> none  [shards(): jnp.full((owners * depth,), -1, jnp.int32).at[flat].set(order_key)]
  transfers between devices with their start and end apart: 2 -> 0, of which waited for: 2 -> 0; matrix products, arithmetic and copies ran while one was open for 2% -> 0% of each run, Pallas kernels for 0% -> 0%
where the time goes in v1:
time: 72.9 us; the launch traced here: 72.8 us
  Pallas kernels  70.1 us (96%)
  other arithmetic  2.06 us (3%)
    pallas_call x1, Pallas kernels, shards(): pl.pallas_call(functools.partial(kernel, rows, width), out_shape=jax.Shap...  70.1 us

profile of v1, /device:TPU:1, one launch (start us, length us, event | category | flops | bytes accessed | tf_op | source)
XLA Modules:
  0.0 72.8 jit_solution(6614718744457193675)
XLA Ops:
  0.0 0.0 copy-start
  0.0 0.7 multiply_reduce_fusion
  0.7 0.0 copy-done
  0.7 0.1 pad_maximum_fusion
  0.8 0.6 reshape.8.meta_in
  1.4 70.1 %shard_map.37 = f32[1,320]{1,0:T(1,128)} custom-call(bf16[320,768]{1,0:T(8,128)(2,1)} %x_ref.1, f32[1,768]{1,0:T(1,128)} %reshape.8.meta_in), custom_call_target="tpu_custom_call" | custom-call | flops 11324620800 | bytes 491520 | tf_op jit(solution)/shard_map/pallas_call | solution.py:301
  71.5 1.3 %reduce.1 = f32[320]{0:T(512)} reduce(f32[1,320]{1,0:T(1,128)} %shard_map.37, f32[]{:T(128)} %constant.8), dimensions={0}, to_apply=%pallas_call.3.reduce_sub_computation | reduce | bytes 2564 | tf_op jit(solution)/shard_map/pallas_call | solution.py:301
  (2 shorter events, 0.0 us)
Async XLA Ops:
  0.0 0.7 copy-start

commit v2 on v0

v2 whole, which is shorter than its diff:
```python
import functools

import jax
import jax.numpy as jnp
from jax import lax
from jax.experimental import pallas as pl
from jax.experimental.pallas import tpu as pltpu
from jax.sharding import PartitionSpec as P

MESH = pl.DeviceIdType.MESH
NT = (((1,), (1,)), ((), ()))
epsilon = 1e-06
scale = 65536.0

OFFSETS = {
    "o": (0, 0, 0), "a": (0, 0, 1), "b": (0, 0, 3), "c": (0, 1, 0),
    "d": (0, 2, 1), "e": (0, 3, 1), "f": (1, 0, 1), "g": (1, 0, 2),
    "h": (2, 0, 1), "i": (3, 1, 0), "j": (3, 1, 3), "k": (3, 2, 0),
}
FULL = "oabcefhijk"
HALF = "dg"
CHUNKS = (80, 80, 80, 80)
ONE_WAY = {"ab", "da", "db", "dh", "gk", "ha", "hb", "oo"}
ROWS_OF = "oabcdefghijk"
COLUMNS_OF = "oabcefij"
PROGRAM = (
    ">oc0", ">oa0", ">ob0", ">oc1", ">oa1", ">ob1", ">oc2", ">oa2", ">ob2", ">oc3", ">oa3", ">ob3", "=o0", "=o1",
    "=o2", "=o3", "!o", "*oo", "?c0", ">ci0", "=c0", "?a0", ">af0", ">ae0", "=a0", "?b0", "=b0", "?c1", ">ci1",
    "=c1", "?a1", ">af1", ">ae1", "=a1", "?b1", "=b1", "?i0", ">ik0", ">ij0", "=i0", "?f0", ">fg0", "=f0", "?e0",
    "=e0", "?c2", ">ci2", "=c2", "?a2", ">af2", ">ae2", "=a2", "?b2", "=b2", "?i1", ">ik1", ">ij1", "=i1", "?f1",
    ">fg1", "=f1", "?e1", "=e1", "?c3", ">ci3", "=c3", "?a3", ">af3", ">ae3", ">fh0", ">ed0", ">fh1", ">ed1", "=a3",
    "?b3", "=b3", "*co", "!c", "*bc", "?i2", ">ik2", ">ij2", "=i2", "?f2", ">fh2", ">fg2", "=f2", "?e2", ">ed2",
    "=e2", "?k0", "=k0", "?g0", "?j0", "=j0", "!b", "*aocb", "?i3", ">ik3", ">ij3", "=i3", "?f3", ">fh3", ">fg3",
    "=f3", "?e3", ">ed3", "=e3", "?k1", "=k1", "?g1", "?j1", "=j1", "!a", "*ioab", "!i", "*fobai", "?h0", "=h0",
    "?d0", "?k2", "=k2", "?g2", "?j2", "=j2", "!f", "*ecibf", "<c", "?h1", "=h1", "?d1", "?k3", "=k3", "?g3", "?j3",
    "=j3", "*kobf", "!e", "*jaef", "<f", "?h2", "=h2", "?d2", "!j", "!k", "*gbejk", "<g", "<k", "?h3", "=h3", "?d3",
    "*hoabei", "<e", "<i", "!h", "*dabhj", "<a", "<b", "<d", "<h", "<j",
)
BLOCKS = FULL + HALF
SLOT = {b: n for n, b in enumerate(BLOCKS)}


def kernel(rows, width, x_ref, cluster_ref, key_ref, out_ref, full, half, meta, col_c, col_g, acc_row, acc_col, ret, back,
           send, recv, d2d_send, d2d_recv, m_send, m_recv, md_send, md_recv, r_send, r_recv):
    x, grid = lax.axis_index("dp"), lax.axis_index("grid")
    y, z, core = grid // 8, (grid // 2) % 4, grid % 2
    pair_rows = 2 * rows
    starts = [sum(CHUNKS[:n]) for n in range(len(CHUNKS))]
    mine = pl.multiple_of(core * rows, 16)

    def device(offset, which):
        dx, dy, dz = offset
        return ((x + dx) % 4, ((y + dy) % 4) * 8 + ((z + dz) % 4) * 2 + which)

    sibling = device((0, 0, 0), 1 - core)
    barrier = pltpu.get_barrier_semaphore()
    partners = {((0, 0, 0), 1)}
    for b in BLOCKS[1:]:
        for offset in (OFFSETS[b], tuple(-v % 4 for v in OFFSETS[b])):
            partners.add((offset, 0))
            if b in FULL:
                partners.add((offset, 1))
    partners = [device(offset, 1 - core if other else core) for offset, other in sorted(partners)]
    for n in partners:
        pl.semaphore_signal(barrier, inc=1, device_id=n, device_id_type=MESH)

    pending = []

    def copy(src, dst, send_sem, recv_sem, to):
        c = pltpu.make_async_remote_copy(
            src_ref=src, dst_ref=dst, send_sem=send_sem, recv_sem=recv_sem, device_id=to, device_id_type=MESH)
        c.start()
        pending.append(c)

    def arrived(here, sem):
        pltpu.make_async_copy(here, here, sem).wait()

    def place(b, s, which):
        if b in FULL:
            return full.at[SLOT[b], pl.ds(pl.multiple_of(which * rows + starts[s], 16), CHUNKS[s])]
        return half.at[SLOT[b] - len(FULL), pl.ds(starts[s], CHUNKS[s])]

    def hop(source, target, s):
        offset = tuple((q - p) % 4 for p, q in zip(OFFSETS[source], OFFSETS[target]))
        a, b, to = SLOT[source], SLOT[target], device(offset, core)
        if s == 0:
            copy(meta.at[a, core], meta.at[b, core], m_send.at[b], m_recv.at[b], to)
        copy(place(source, s, core), place(target, s, core), send.at[b, s], recv.at[b, s], to)

    def got(b, s):
        n = SLOT[b]
        if s == 0:
            arrived(meta.at[n, core], m_recv.at[n])
        arrived(place(b, s, core), recv.at[n, s])

    def share(b, s):
        n = SLOT[b]
        if s == 0:
            copy(meta.at[n, core], meta.at[n, core], md_send.at[n], md_recv.at[n], sibling)
        copy(place(b, s, core), place(b, s, core), d2d_send.at[n, s], d2d_recv.at[n, s], sibling)

    def shared(b):
        n = SLOT[b]
        arrived(meta.at[n, 1 - core], md_recv.at[n])
        for s in range(len(CHUNKS)):
            arrived(place(b, s, 1 - core), d2d_recv.at[n, s])

    def columns(b):
        r = meta[SLOT[b], core]
        r = r[:, 0:384] + r[:, 320:704]
        t = jnp.transpose(jnp.broadcast_to(r, (128, 384)))[:rows]
        col_g[SLOT[b]] = t
        col_c[SLOT[b]] = jnp.floor(t * (1.0 / scale))

    def tiles(j, others):
        left = full[SLOT[j], pl.ds(mine, rows), :] if j in FULL else half[SLOT[j] - len(FULL)]
        cj, gj = col_c[SLOT[j]], col_g[SLOT[j]]
        best = acc_row[SLOT[j]]
        for i in others:
            sims = lax.dot_general(left, full[SLOT[i]], NT, preferred_element_type=jnp.float32)
            gi = meta[SLOT[i], 0] + meta[SLOT[i], 1]
            ci = jnp.floor(gi * (1.0 / scale))
            for n in range(0, pair_rows, 128):
                t = jnp.where(cj == ci[:, n:n + 128], sims[:, n:n + 128], -1.0)
                earlier = gi[:, n:n + 128] < gj
                best = jnp.maximum(best, jnp.where(earlier, t, -1.0))
                if j + i not in ONE_WAY:
                    u = jnp.max(jnp.where(earlier, -1.0, t).reshape(rows // 8, 8, 128), axis=0)
                    acc_col[SLOT[i], :, n:n + 128] = jnp.maximum(acc_col[SLOT[i], :, n:n + 128], u)
        acc_row[SLOT[j]] = best

    lanes = lax.broadcasted_iota(jnp.int32, (1, pair_rows), 1)
    ours = (lanes >= core * rows) & (lanes < (core + 1) * rows)

    def summary(b):
        m = jnp.full((1, pair_rows), -1.0, jnp.float32)
        if b in ROWS_OF:
            a = jnp.concatenate([acc_row[SLOT[b]], jnp.full((384 - rows, 128), -1.0, jnp.float32)], axis=0)
            r = jnp.max(jnp.transpose(a), axis=0, keepdims=True)[:, :rows]
            m = jnp.where(ours, jnp.concatenate([r, r], axis=1), m)
        if b in COLUMNS_OF:
            m = jnp.maximum(m, jnp.max(acc_col[SLOT[b]], axis=0, keepdims=True))
        return m

    def owners(b):
        return (1,) if b == "o" else (0, 1) if b in COLUMNS_OF else (0,)

    def give(b):
        n = SLOT[b]
        back[n] = summary(b)
        home = tuple(-v for v in OFFSETS[b])
        for which in owners(b):
            copy(back.at[n], ret.at[which, n], r_send.at[which, n], r_recv.at[which, n],
                 device(home, 1 - core if which else core))

    values = x_ref[...].astype(jnp.float32)
    units = values * lax.rsqrt(jnp.sum(values * values, axis=1, keepdims=True) + epsilon)
    full[0, pl.ds(mine, rows), :] = units.astype(jnp.bfloat16)
    wide = lax.broadcasted_iota(jnp.int32, (1, 768), 1)
    own = (cluster_ref[...] * 65536 + key_ref[...].reshape(1, rows)).astype(jnp.float32)
    own = jnp.concatenate([own, own, jnp.zeros((1, 768 - 2 * rows), jnp.float32)], axis=1)
    meta[0, core] = jnp.where((wide >= core * rows) & (wide < (core + 1) * rows), own, 0.0)
    pl.semaphore_wait(barrier, len(partners))

    known = set()
    for token in PROGRAM:
        what, b = token[0], token[1]
        if what == ">":
            hop(b, token[2], int(token[3]))
        elif what == "?":
            got(b, int(token[2]))
        elif what == "=":
            share(b, int(token[2]))
        elif what == "!":
            if b == "o":
                acc_row[...] = jnp.full_like(acc_row, -1.0)
                acc_col[...] = jnp.full_like(acc_col, -1.0)
            shared(b)
        elif what == "*":
            if b not in known:
                columns(b)
                known.add(b)
            tiles(b, token[2:])
        else:
            give(b)
    if "o" in COLUMNS_OF:
        give("o")
    total = back[0]
    for c in pending:
        c.wait_send()
    for b in BLOCKS:
        for which in owners(b):
            arrived(ret.at[which, SLOT[b]], r_recv.at[which, SLOT[b]])
            total = jnp.maximum(total, ret[which, SLOT[b]])
    out_ref[...] = jnp.where(core == 0, total[:, :rows], total[:, rows:]).reshape(rows)


def shards(embeddings, cluster, order_key):
    rows, width = embeddings.shape
    nf, nh, nb, nc = len(FULL), len(HALF), len(BLOCKS), len(CHUNKS)
    dma = pltpu.SemaphoreType.DMA
    return pl.pallas_call(
        functools.partial(kernel, rows, width),
        out_shape=jax.ShapeDtypeStruct((rows,), jnp.float32),
        in_specs=[pl.BlockSpec(memory_space=pltpu.VMEM)] * 3,
        out_specs=pl.BlockSpec(memory_space=pltpu.VMEM),
        scratch_shapes=[
            pltpu.VMEM((nf, 2 * rows, width), jnp.bfloat16),
            pltpu.VMEM((nh, rows, width), jnp.bfloat16),
            pltpu.VMEM((nb, 2, 1, 768), jnp.float32),
            pltpu.VMEM((nb, rows, 128), jnp.float32),
            pltpu.VMEM((nb, rows, 128), jnp.float32),
            pltpu.VMEM((nb, rows, 128), jnp.float32),
            pltpu.VMEM((nf, 8, 2 * rows), jnp.float32),
            pltpu.VMEM((2, nb, 1, 2 * rows), jnp.float32),
            pltpu.VMEM((nb, 1, 2 * rows), jnp.float32),
            dma((nb, nc)), dma((nb, nc)), dma((nf, nc)), dma((nf, nc)),
            dma((nb,)), dma((nb,)), dma((nf,)), dma((nf,)), dma((2, nb)), dma((2, nb)),
        ],
        compiler_params=pltpu.CompilerParams(
            collective_id=0, has_side_effects=True, vmem_limit_bytes=56 << 20),
        cost_estimate=pl.CostEstimate(
            flops=36 * 2 * rows * 2 * rows * width, bytes_accessed=rows * width * 2, transcendentals=rows),
    )(embeddings, cluster.reshape(1, rows), order_key)


def solution(mesh):
    placed = (P(("dp", "grid"), None), P(("dp", "grid"), None), P(("dp", "grid")))
    return jax.shard_map(
        shards, mesh=mesh, in_specs=placed, out_specs=P(("dp", "grid")), check_vma=False
    )
```

time: 190 us -> 53.1 us (0.28)
  waiting for transfers between devices: 76.5 us -> 0 us
  blocking collectives: 53.4 us -> 0 us
  Pallas kernels: 0 us -> 51.7 us
  matrix products: 27.4 us -> 0 us
  between operations: 13.5 us -> 0.01 us
  other arithmetic: 7.01 us -> 0 us
  local copies, waits for them, and re-layouts: 7.11 us -> 1.26 us
  starting transfers between devices: 3.96 us -> 0 us
    all_gather x1 -> x0, waiting for transfers between devices: 72.4 us -> none  [shards(): other_units = lax.all_gather(mine, 'grid', axis=0, tiled=True)]
    pallas_call x0 -> x1, Pallas kernels: none -> 51.7 us  [shards(): pl.pallas_call(functools.partial(kernel, rows, width), out_shape=jax.Shap...]
    all_gather x1 -> x0, blocking collectives: 29 us -> none  [shards(): other_keys = lax.all_gather(mine_keys, 'grid', axis=0, tiled=True)]
    dot_general x1 -> x0, matrix products: 27.4 us -> none  [shards(): jnp.einsum('qe,ke->qk', mine, other_units, preferred_element_type=jnp.flo...]
    all_to_all x2 -> x0, blocking collectives: 24.4 us -> none  [the longest x1 17.9 us: shards(): lax.all_to_all(send_units, 'dp', split_axis=0, concat_axis=0, tiled=True)]
    all_to_all x1 -> x0, waiting for transfers between devices: 4.13 us -> none  [shards(): lax.all_to_all(scores.reshape(owners, depth), 'dp', split_axis=0, concat_...]
    all_to_all x1 -> x0, starting transfers between devices: 3.96 us -> none  [shards(): lax.all_to_all(scores.reshape(owners, depth), 'dp', split_axis=0, concat_...]
    scatter x1 -> x0, local copies, waits for them, and re-layouts: 3.08 us -> none  [shards(): jnp.full((owners * depth,), -1, jnp.int32).at[flat].set(order_key)]
  transfers between devices with their start and end apart: 2 -> 0, of which waited for: 2 -> 0; matrix products, arithmetic and copies ran while one was open for 2% -> 0% of each run, Pallas kernels for 0% -> 0%
where the time goes in v2:
time: 53.1 us; the launch traced here: 52.9 us
  Pallas kernels  51.7 us (97%)
  local copies, waits for them, and re-layouts  1.26 us (2%)
    pallas_call x1, Pallas kernels, shards(): pl.pallas_call(functools.partial(kernel, rows, width), out_shape=jax.Shap...  51.7 us
    unnamed x1, local copies, waits for them, and re-layouts  1.26 us

profile of v2, /device:TPU:1, one launch (start us, length us, event | category | flops | bytes accessed | tf_op | source)
XLA Modules:
  0.0 52.9 jit_solution(14186494393158311678)
XLA Ops:
  0.0 51.7 %shard_map.37 = f32[320]{0:T(512)} custom-call(bf16[320,768]{1,0:T(8,128)(2,1)} %x_ref.1, s32[1,320]{1,0:T(1,128)} %bitcast.1, s32[320]{0:T(512)} %key_ref.1), custom_call_target="tpu_custom_call" | custom-call | flops 11324620800 | bytes 491520 | tf_op jit(solution)/shard_map/pallas_call | solution.py:202
  51.7 1.3 %copy.5 = f32[320]{0:T(512)} copy(f32[320]{0:T(512)} %shard_map.37) | data formatting | bytes 2560

commit v3 on v2

--- a/solution.py
+++ b/solution.py
@@ -40,7 +40,7 @@
 SLOT = {b: n for n, b in enumerate(BLOCKS)}
 
 
-def kernel(rows, width, x_ref, cluster_ref, key_ref, out_ref, full, half, meta, col_c, col_g, acc_row, acc_col, ret, back,
+def kernel(rows, width, x_hbm, cluster_ref, key_ref, out_ref, x_ref, x_sem, full, half, meta, col_c, col_g, acc_row, acc_col, ret, back,
            send, recv, d2d_send, d2d_recv, m_send, m_recv, md_send, md_recv, r_send, r_recv):
     x, grid = lax.axis_index("dp"), lax.axis_index("grid")
     y, z, core = grid // 8, (grid // 2) % 4, grid % 2
@@ -53,6 +53,8 @@
         return ((x + dx) % 4, ((y + dy) % 4) * 8 + ((z + dz) % 4) * 2 + which)
 
     sibling = device((0, 0, 0), 1 - core)
+    load = pltpu.make_async_copy(x_hbm, x_ref, x_sem)
+    load.start()
     barrier = pltpu.get_barrier_semaphore()
     partners = {((0, 0, 0), 1)}
     for b in BLOCKS[1:]:
@@ -116,13 +118,17 @@
         left = full[SLOT[j], pl.ds(mine, rows), :] if j in FULL else half[SLOT[j] - len(FULL)]
         cj, gj = col_c[SLOT[j]], col_g[SLOT[j]]
         best = acc_row[SLOT[j]]
-        for i in others:
-            sims = lax.dot_general(left, full[SLOT[i]], NT, preferred_element_type=jnp.float32)
-            gi = meta[SLOT[i], 0] + meta[SLOT[i], 1]
-            ci = jnp.floor(gi * (1.0 / scale))
-            for n in range(0, pair_rows, 128):
-                t = jnp.where(cj == ci[:, n:n + 128], sims[:, n:n + 128], -1.0)
-                earlier = gi[:, n:n + 128] < gj
+        keys = {i: meta[SLOT[i], 0] + meta[SLOT[i], 1] for i in others}
+        groups = {i: jnp.floor(keys[i] * (1.0 / scale)) for i in others}
+        units = [(i, n) for i in others for n in range(0, pair_rows, 128)]
+        for first in range(0, len(units), 2):
+            some = units[first:first + 2]
+            right = [full[SLOT[i], n:n + 128, :] for i, n in some]
+            right = right[0] if len(some) == 1 else jnp.concatenate(right, axis=0)
+            sims = lax.dot_general(left, right, NT, preferred_element_type=jnp.float32)
+            for at, (i, n) in enumerate(some):
+                t = jnp.where(cj == groups[i][:, n:n + 128], sims[:, at * 128:at * 128 + 128], -1.0)
+                earlier = keys[i][:, n:n + 128] < gj
                 best = jnp.maximum(best, jnp.where(earlier, t, -1.0))
                 if j + i not in ONE_WAY:
                     u = jnp.max(jnp.where(earlier, -1.0, t).reshape(rows // 8, 8, 128), axis=0)
@@ -153,6 +159,7 @@
             copy(back.at[n], ret.at[which, n], r_send.at[which, n], r_recv.at[which, n],
                  device(home, 1 - core if which else core))
 
+    load.wait()
     values = x_ref[...].astype(jnp.float32)
     units = values * lax.rsqrt(jnp.sum(values * values, axis=1, keepdims=True) + epsilon)
     full[0, pl.ds(mine, rows), :] = units.astype(jnp.bfloat16)
@@ -202,9 +209,11 @@
     return pl.pallas_call(
         functools.partial(kernel, rows, width),
         out_shape=jax.ShapeDtypeStruct((rows,), jnp.float32),
-        in_specs=[pl.BlockSpec(memory_space=pltpu.VMEM)] * 3,
+        in_specs=[pl.BlockSpec(memory_space=pl.ANY)] + [pl.BlockSpec(memory_space=pltpu.VMEM)] * 2,
         out_specs=pl.BlockSpec(memory_space=pltpu.VMEM),
         scratch_shapes=[
+            pltpu.VMEM((rows, width), jnp.bfloat16),
+            pltpu.SemaphoreType.DMA,
             pltpu.VMEM((nf, 2 * rows, width), jnp.bfloat16),
             pltpu.VMEM((nh, rows, width), jnp.bfloat16),
             pltpu.VMEM((nb, 2, 1, 768), jnp.float32),

time: 53.1 us -> 51.3 us (0.966)
  Pallas kernels: 51.7 us -> 49.8 us
    pallas_call x1, Pallas kernels: 51.7 us -> 49.8 us  [shards(): pl.pallas_call(functools.partial(kernel, rows, width), out_shape=jax.Shap...]
where the time goes in v3:
time: 51.3 us; the launch traced here: 51.1 us
  Pallas kernels  49.8 us (97%)
  local copies, waits for them, and re-layouts  1.26 us (2%)
    pallas_call x1, Pallas kernels, shards(): pl.pallas_call(functools.partial(kernel, rows, width), out_shape=jax.Shap...  49.8 us
    unnamed x1, local copies, waits for them, and re-layouts  1.26 us

profile of v3, /device:TPU:1, one launch (start us, length us, event | category | flops | bytes accessed | tf_op | source)
XLA Modules:
  0.0 51.1 jit_solution(11652798646374025625)
XLA Ops:
  0.0 49.8 %shard_map.37 = f32[320]{0:T(512)} custom-call(bf16[320,768]{1,0:T(8,128)(2,1)} %x_hbm.1, s32[1,320]{1,0:T(1,128)} %bitcast.1, s32[320]{0:T(512)} %key_ref.1), custom_call_target="tpu_custom_call" | custom-call | flops 11324620800 | bytes 491520 | tf_op jit(solution)/shard_map/pallas_call | solution.py:209
  49.8 1.3 %copy.5 = f32[320]{0:T(512)} copy(f32[320]{0:T(512)} %shard_map.37) | data formatting | bytes 2560

commit v4 on v3

--- a/solution.py
+++ b/solution.py
@@ -38,9 +38,15 @@
 )
 BLOCKS = FULL + HALF
 SLOT = {b: n for n, b in enumerate(BLOCKS)}
-
-
-def kernel(rows, width, x_hbm, cluster_ref, key_ref, out_ref, x_ref, x_sem, full, half, meta, col_c, col_g, acc_row, acc_col, ret, back,
+CROSSED = sorted(ONE_WAY - {"oo"})
+COLUMNS = COLUMNS_OF + "".join(sorted({i for _, i in CROSSED} - set(COLUMNS_OF)))
+
+
+def between(source, target):
+    return tuple((q - p) % 4 for p, q in zip(OFFSETS[source], OFFSETS[target]))
+
+
+def kernel(rows, width, x_hbm, cluster_ref, key_ref, out_ref, x_ref, x_sem, full, half, meta, col_c, col_g, acc_row, acc_col, acc_cross, ret, back,
            send, recv, d2d_send, d2d_recv, m_send, m_recv, md_send, md_recv, r_send, r_recv):
     x, grid = lax.axis_index("dp"), lax.axis_index("grid")
     y, z, core = grid // 8, (grid // 2) % 4, grid % 2
@@ -57,10 +63,14 @@
     load.start()
     barrier = pltpu.get_barrier_semaphore()
     partners = {((0, 0, 0), 1)}
+    for token in PROGRAM:
+        if token[0] == ">":
+            offset = between(token[1], token[2])
+            partners |= {(offset, 0), (tuple(-v % 4 for v in offset), 0)}
     for b in BLOCKS[1:]:
         for offset in (OFFSETS[b], tuple(-v % 4 for v in OFFSETS[b])):
             partners.add((offset, 0))
-            if b in FULL:
+            if b in COLUMNS:
                 partners.add((offset, 1))
     partners = [device(offset, 1 - core if other else core) for offset, other in sorted(partners)]
     for n in partners:
@@ -83,8 +93,7 @@
         return half.at[SLOT[b] - len(FULL), pl.ds(starts[s], CHUNKS[s])]
 
     def hop(source, target, s):
-        offset = tuple((q - p) % 4 for p, q in zip(OFFSETS[source], OFFSETS[target]))
-        a, b, to = SLOT[source], SLOT[target], device(offset, core)
+        a, b, to = SLOT[source], SLOT[target], device(between(source, target), core)
         if s == 0:
             copy(meta.at[a, core], meta.at[b, core], m_send.at[b], m_recv.at[b], to)
         copy(place(source, s, core), place(target, s, core), send.at[b, s], recv.at[b, s], to)
@@ -114,25 +123,43 @@
         col_g[SLOT[b]] = t
         col_c[SLOT[b]] = jnp.floor(t * (1.0 / scale))
 
+    low = lax.broadcasted_iota(jnp.int32, (1, 384), 1) < rows
+
+    def turn(j, i):
+        d = between(j, i)
+        return (x if d[0] == 2 else y if d[1] == 2 else z) // 2
+
     def tiles(j, others):
         left = full[SLOT[j], pl.ds(mine, rows), :] if j in FULL else half[SLOT[j] - len(FULL)]
         cj, gj = col_c[SLOT[j]], col_g[SLOT[j]]
         best = acc_row[SLOT[j]]
         keys = {i: meta[SLOT[i], 0] + meta[SLOT[i], 1] for i in others}
         groups = {i: jnp.floor(keys[i] * (1.0 / scale)) for i in others}
-        units = [(i, n) for i in others for n in range(0, pair_rows, 128)]
+        cross = {i: j + i in ONE_WAY and i != j for i in others}
+        side = {i: lax.rem(core + turn(j, i), 2) for i in others if cross[i]}
+        for i in side:
+            r = meta[SLOT[i], side[i]]
+            keys[i] = jnp.where(low, r[:, 0:384] + r[:, 320:704], -scale)
+            groups[i] = jnp.floor(keys[i] * (1.0 / scale))
+        units = [(i, n) for i in others for n in ((0, 128, rows - 128) if cross[i] else range(0, pair_rows, 128))]
         for first in range(0, len(units), 2):
             some = units[first:first + 2]
-            right = [full[SLOT[i], n:n + 128, :] for i, n in some]
+            right = [
+                full[SLOT[i], pl.ds(pl.multiple_of(side[i] * rows + n, 16), 128), :] if cross[i]
+                else full[SLOT[i], n:n + 128, :] for i, n in some]
             right = right[0] if len(some) == 1 else jnp.concatenate(right, axis=0)
             sims = lax.dot_general(left, right, NT, preferred_element_type=jnp.float32)
             for at, (i, n) in enumerate(some):
                 t = jnp.where(cj == groups[i][:, n:n + 128], sims[:, at * 128:at * 128 + 128], -1.0)
                 earlier = keys[i][:, n:n + 128] < gj
                 best = jnp.maximum(best, jnp.where(earlier, t, -1.0))
-                if j + i not in ONE_WAY:
+                if i != j:
                     u = jnp.max(jnp.where(earlier, -1.0, t).reshape(rows // 8, 8, 128), axis=0)
-                    acc_col[SLOT[i], :, n:n + 128] = jnp.maximum(acc_col[SLOT[i], :, n:n + 128], u)
+                    if cross[i]:
+                        at_ = {0: 0, 128: 128, rows - 128: 256}[n]
+                        acc_cross[CROSSED.index(j + i), :, at_:at_ + 128] = u
+                    else:
+                        acc_col[SLOT[i], :, n:n + 128] = jnp.maximum(acc_col[SLOT[i], :, n:n + 128], u)
         acc_row[SLOT[j]] = best
 
     lanes = lax.broadcasted_iota(jnp.int32, (1, pair_rows), 1)
@@ -146,10 +173,19 @@
             m = jnp.where(ours, jnp.concatenate([r, r], axis=1), m)
         if b in COLUMNS_OF:
             m = jnp.maximum(m, jnp.max(acc_col[SLOT[b]], axis=0, keepdims=True))
+        for n, (j, i) in enumerate(CROSSED):
+            if i == b:
+                r = jnp.max(acc_cross[n], axis=0, keepdims=True)
+                r = jnp.concatenate([
+                    r[:, :rows - 128], jnp.maximum(r[:, rows - 128:256], r[:, 256:512 - (rows - 128)]),
+                    r[:, 256 + 256 - (rows - 128):384]], axis=1)
+                side = lax.rem(core + turn(j, i), 2)
+                there = (lanes >= side * rows) & (lanes < (side + 1) * rows)
+                m = jnp.where(there, jnp.maximum(m, jnp.concatenate([r, r], axis=1)), m)
         return m
 
     def owners(b):
-        return (1,) if b == "o" else (0, 1) if b in COLUMNS_OF else (0,)
+        return (1,) if b == "o" else (0, 1) if b in COLUMNS else (0,)
 
     def give(b):
         n = SLOT[b]
@@ -190,7 +226,7 @@
             tiles(b, token[2:])
         else:
             give(b)
-    if "o" in COLUMNS_OF:
+    if "o" in COLUMNS:
         give("o")
     total = back[0]
     for c in pending:
@@ -221,6 +257,7 @@
             pltpu.VMEM((nb, rows, 128), jnp.float32),
             pltpu.VMEM((nb, rows, 128), jnp.float32),
             pltpu.VMEM((nf, 8, 2 * rows), jnp.float32),
+            pltpu.VMEM((len(CROSSED), 8, 384), jnp.float32),
             pltpu.VMEM((2, nb, 1, 2 * rows), jnp.float32),
             pltpu.VMEM((nb, 1, 2 * rows), jnp.float32),
             dma((nb, nc)), dma((nb, nc)), dma((nf, nc)), dma((nf, nc)),

time: 51.3 us -> 51 us (level)
  no operation moved by 1% of the time
where the time goes in v4:
time: 51 us; the launch traced here: 50.8 us
  Pallas kernels  49.5 us (97%)
  local copies, waits for them, and re-layouts  1.26 us (2%)
    pallas_call x1, Pallas kernels, shards(): pl.pallas_call(functools.partial(kernel, rows, width), out_shape=jax.Shap...  49.5 us
    unnamed x1, local copies, waits for them, and re-layouts  1.26 us

profile of v4, /device:TPU:1, one launch (start us, length us, event | category | flops | bytes accessed | tf_op | source)
XLA Modules:
  0.0 50.8 jit_solution(13664787967802989232)
XLA Ops:
  0.0 49.5 %shard_map.37 = f32[320]{0:T(512)} custom-call(bf16[320,768]{1,0:T(8,128)(2,1)} %x_hbm.1, s32[1,320]{1,0:T(1,128)} %bitcast.1, s32[320]{0:T(512)} %key_ref.1), custom_call_target="tpu_custom_call" | custom-call | flops 11324620800 | bytes 491520 | tf_op jit(solution)/shard_map/pallas_call | solution.py:245
  49.5 1.3 %copy.5 = f32[320]{0:T(512)} copy(f32[320]{0:T(512)} %shard_map.37) | data formatting | bytes 2560

commit v5 on v4

--- a/solution.py
+++ b/solution.py
@@ -13,28 +13,30 @@
 scale = 65536.0
 
 OFFSETS = {
-    "o": (0, 0, 0), "a": (0, 0, 1), "b": (0, 0, 3), "c": (0, 1, 0),
-    "d": (0, 2, 1), "e": (0, 3, 1), "f": (1, 0, 1), "g": (1, 0, 2),
-    "h": (2, 0, 1), "i": (3, 1, 0), "j": (3, 1, 3), "k": (3, 2, 0),
+    "o": (0, 0, 0), "a": (0, 0, 3), "b": (0, 1, 0), "c": (0, 3, 0),
+    "d": (0, 3, 1), "e": (0, 3, 2), "f": (1, 0, 0), "g": (1, 1, 0),
+    "h": (2, 1, 0), "i": (3, 0, 2), "j": (3, 0, 3), "k": (3, 1, 3),
 }
-FULL = "oabcefhijk"
-HALF = "dg"
-CHUNKS = (80, 80, 80, 80)
-ONE_WAY = {"ab", "da", "db", "dh", "gk", "ha", "hb", "oo"}
+FULL = "oabcdfghj"
+HALF = "eik"
+CHUNKS = (64, 64, 64, 64, 64)
+ONE_WAY = {"bc", "eb", "ec", "eh", "hb", "hc", "if", "oo"}
 ROWS_OF = "oabcdefghijk"
-COLUMNS_OF = "oabcefij"
+COLUMNS_OF = "oabcdfghj"
 PROGRAM = (
-    ">oc0", ">oa0", ">ob0", ">oc1", ">oa1", ">ob1", ">oc2", ">oa2", ">ob2", ">oc3", ">oa3", ">ob3", "=o0", "=o1",
-    "=o2", "=o3", "!o", "*oo", "?c0", ">ci0", "=c0", "?a0", ">af0", ">ae0", "=a0", "?b0", "=b0", "?c1", ">ci1",
-    "=c1", "?a1", ">af1", ">ae1", "=a1", "?b1", "=b1", "?i0", ">ik0", ">ij0", "=i0", "?f0", ">fg0", "=f0", "?e0",
-    "=e0", "?c2", ">ci2", "=c2", "?a2", ">af2", ">ae2", "=a2", "?b2", "=b2", "?i1", ">ik1", ">ij1", "=i1", "?f1",
-    ">fg1", "=f1", "?e1", "=e1", "?c3", ">ci3", "=c3", "?a3", ">af3", ">ae3", ">fh0", ">ed0", ">fh1", ">ed1", "=a3",
-    "?b3", "=b3", "*co", "!c", "*bc", "?i2", ">ik2", ">ij2", "=i2", "?f2", ">fh2", ">fg2", "=f2", "?e2", ">ed2",
-    "=e2", "?k0", "=k0", "?g0", "?j0", "=j0", "!b", "*aocb", "?i3", ">ik3", ">ij3", "=i3", "?f3", ">fh3", ">fg3",
-    "=f3", "?e3", ">ed3", "=e3", "?k1", "=k1", "?g1", "?j1", "=j1", "!a", "*ioab", "!i", "*fobai", "?h0", "=h0",
-    "?d0", "?k2", "=k2", "?g2", "?j2", "=j2", "!f", "*ecibf", "<c", "?h1", "=h1", "?d1", "?k3", "=k3", "?g3", "?j3",
-    "=j3", "*kobf", "!e", "*jaef", "<f", "?h2", "=h2", "?d2", "!j", "!k", "*gbejk", "<g", "<k", "?h3", "=h3", "?d3",
-    "*hoabei", "<e", "<i", "!h", "*dabhj", "<a", "<b", "<d", "<h", "<j",
+    ">of3", ">oc4", ">ob0", ">of2", ">oc0", ">of4", ">oa0", ">oc1", ">ob1", ">ob2", ">oa1", ">oa2", "=o0", "=o1",
+    "=o2", "=o3", "=o4", "!o", "*oo", "?f3", "=f3", "?c4", ">cd4", ">oc2", "=c4", "?b0", ">ob3", ">bg0", "=b0",
+    "?a0", ">aj0", ">oa3", "=a0", "?f2", "=f2", "?c0", ">cd0", ">oc3", "=c0", "?b1", ">bg1", ">fg3", "=b1", "?a1",
+    ">aj1", ">oa4", "=a1", "?f4", "=f4", "?c1", ">cd1", "=c1", "?b2", ">bg2", ">fg4", "=b2", "?d4", ">de4", "=d4",
+    "?a2", ">aj2", "=a2", "?j0", ">ji0", "=j0", "?g0", ">gf0", ">gh0", "=g0", "?c2", "=c2", "?b3", ">jk0", "=b3",
+    "?d0", ">cd2", "=d0", "?a3", ">aj3", "=a3", "?j1", ">ji1", "=j1", "?g1", ">gf1", ">gh1", "=g1", "?c3", "=c3",
+    "?d1", ">cd3", "=d1", "?g3", ">jk1", "=g3", "?a4", ">aj4", "=a4", "?j2", ">ji2", "=j2", "*co", "!c", "*aoc",
+    "?g2", ">gh2", "=g2", "?f0", "=f0", "?e4", ">de1", "?g4", ">gb4", ">jk2", "=g4", "?i0", "?j3", ">ji3", "=j3",
+    "!a", "*goac", "?h0", ">gh3", "=h0", "?f1", "=f1", "?d2", ">de2", "=d2", "?k0", ">jk3", "?i1", "?j4", ">ji4",
+    "=j4", "*foa", "!f", "!g", "*jcfg", "?h1", ">gh4", "=h1", "?d3", ">de3", "=d3", "?k1", ">jk4", "?i2", "?b4",
+    "=b4", "!j", "*dafgj", "<j", "?h2", "=h2", "?e1", ">de0", "?k2", "?i3", "!d", "*bacdf", "<a", "?h3", "=h3",
+    "?e2", "?k3", "?i4", "!b", "*iobdfg", "<i", "<g", "?h4", "=h4", "?e3", "?k4", "*hbocd", "!h", "*khcdf", "<k",
+    "<d", "<f", "?e0", "*ecbh", "<e", "<h", "<b", "<c",
 )
 BLOCKS = FULL + HALF
 SLOT = {b: n for n, b in enumerate(BLOCKS)}

time: 51 us -> 50.4 us (0.988)
  Pallas kernels: 49.5 us -> 48.9 us
    pallas_call x1, Pallas kernels: 49.5 us -> 48.9 us  [shards(): pl.pallas_call(functools.partial(kernel, rows, width), out_shape=jax.Shap...]
where the time goes in v5:
time: 50.4 us; the launch traced here: 50.2 us
  Pallas kernels  48.9 us (97%)
  local copies, waits for them, and re-layouts  1.26 us (2%)
    pallas_call x1, Pallas kernels, shards(): pl.pallas_call(functools.partial(kernel, rows, width), out_shape=jax.Shap...  48.9 us
    unnamed x1, local copies, waits for them, and re-layouts  1.26 us

profile of v5, /device:TPU:1, one launch (start us, length us, event | category | flops | bytes accessed | tf_op | source)
XLA Modules:
  0.0 50.2 jit_solution(8397894604389250138)
XLA Ops:
  0.0 48.9 %shard_map.37 = f32[320]{0:T(512)} custom-call(bf16[320,768]{1,0:T(8,128)(2,1)} %x_hbm.1, s32[1,320]{1,0:T(1,128)} %bitcast.1, s32[320]{0:T(512)} %key_ref.1), custom_call_target="tpu_custom_call" | custom-call | flops 11324620800 | bytes 491520 | tf_op jit(solution)/shard_map/pallas_call | solution.py:247
  48.9 1.3 %copy.5 = f32[320]{0:T(512)} copy(f32[320]{0:T(512)} %shard_map.37) | data formatting | bytes 2560

commit v6 on v5

--- a/solution.py
+++ b/solution.py
@@ -134,7 +134,7 @@
     def tiles(j, others):
         left = full[SLOT[j], pl.ds(mine, rows), :] if j in FULL else half[SLOT[j] - len(FULL)]
         cj, gj = col_c[SLOT[j]], col_g[SLOT[j]]
-        best = acc_row[SLOT[j]]
+        best = jnp.full((rows, 128), -1.0, jnp.float32)
         keys = {i: meta[SLOT[i], 0] + meta[SLOT[i], 1] for i in others}
         groups = {i: jnp.floor(keys[i] * (1.0 / scale)) for i in others}
         cross = {i: j + i in ONE_WAY and i != j for i in others}
@@ -218,7 +218,6 @@
             share(b, int(token[2]))
         elif what == "!":
             if b == "o":
-                acc_row[...] = jnp.full_like(acc_row, -1.0)
                 acc_col[...] = jnp.full_like(acc_col, -1.0)
             shared(b)
         elif what == "*":

time: 50.4 us -> 50.4 us (level)
  no operation moved by 1% of the time
where the time goes in v6:
time: 50.4 us; the launch traced here: 50.2 us
  Pallas kernels  48.9 us (97%)
  local copies, waits for them, and re-layouts  1.26 us (2%)
    pallas_call x1, Pallas kernels, shards(): pl.pallas_call(functools.partial(kernel, rows, width), out_shape=jax.Shap...  48.9 us
    unnamed x1, local copies, waits for them, and re-layouts  1.26 us

profile of v6, /device:TPU:1, one launch (start us, length us, event | category | flops | bytes accessed | tf_op | source)
XLA Modules:
  0.0 50.2 jit_solution(8397894604389250138)
XLA Ops:
  0.0 48.9 %shard_map.37 = f32[320]{0:T(512)} custom-call(bf16[320,768]{1,0:T(8,128)(2,1)} %x_hbm.1, s32[1,320]{1,0:T(1,128)} %bitcast.1, s32[320]{0:T(512)} %key_ref.1), custom_call_target="tpu_custom_call" | custom-call | flops 11324620800 | bytes 491520 | tf_op jit(solution)/shard_map/pallas_call | solution.py:246
  48.9 1.3 %copy.5 = f32[320]{0:T(512)} copy(f32[320]{0:T(512)} %shard_map.37) | data formatting | bytes 2560
